TPU v7x, 512 devices: a whole 4x4x16 slice. The times are simulated.
512 devices in a mesh: dp: 16 (over z), expert: 32 (over y, x, core).
Axes of the slice: x: 4, y: 4, z: 16, core: 2. Of those that a mesh axis runs over, the one named last changes fastest.
Arguments:
- tokens: bfloat16 [65536, 1024], P(('dp', 'expert')), may hold values from -6 to 6
- grad_out: bfloat16 [65536, 1024], P(('dp', 'expert')), may hold values from -6 to 6
- expert_ids: int32 [65536, 2], P(('dp', 'expert')), may hold values from 0 to 31, all different within a row; in each aligned block of 128 rows (0 to 127, 128 to 255, ...) at most 16 rows name the same one
- route_probs: bfloat16 [65536, 2], P(('dp', 'expert')), may hold values from 0.19921875 to 1
- gate_up_weight: bfloat16 [1024, 32, 1536], P('dp', 'expert'), may hold values from -0.1875 to 0.1875
- down_weight: bfloat16 [32, 768, 1024], P('expert'), may hold values from -0.21875 to 0.21875
- gate_up_scale_index: int32 [8, 32, 2], P(None, 'expert'), may hold values from 0 to 15
- down_scale_index: int32 [32, 6], P('expert'), may hold values from 0 to 15
- scale_table: float32 [16], replicated, may hold values from 0.5 to 2
Outputs:
- token_grad: bfloat16 [65536, 1024], P(('dp', 'expert'))
- prob_grad: float32 [65536, 2], P(('dp', 'expert'))
- gate_up_grad: bfloat16 [1024, 32, 1536], P('dp', 'expert')
- down_grad: bfloat16 [32, 768, 1024], P('expert')
Inputs may be any that keep to these rules, and one draw needn't show every extreme that they name: `expert_ids`: each row names two different experts. The 128 rows of one device name one expert at most 16 times, and in every draw some device's rows name some expert exactly 16 times.
All inputs are finite; a program needn't handle non-finite values.
Results may differ from a plain program's by a relative error of at most 0.022.
Values may be sent and summed in bfloat16 or wider, within the bound.
No kernel may reach another device: no remote copies, remote signals or barrier semaphores. Data moves between devices by JAX's collectives and lax.ppermute only.
A program may use at most 64 MiB of HBM per device.

v0:
```python
import jax
import jax.numpy as jnp
from jax import lax
from jax.sharding import PartitionSpec as P

QBLOCK = 128


def lookup(level_index, level_table):
    onehot = (level_index[..., None] == jnp.arange(level_table.shape[0], dtype=jnp.int32)).astype(
        level_table.dtype
    )
    return jnp.sum(onehot * level_table, axis=-1)


def slot_tables(routes, experts, capacity):
    flat_routes = routes.reshape(-1)
    expert_hits = (flat_routes[:, None] == jnp.arange(experts, dtype=jnp.int32)[None, :]).astype(
        jnp.int32
    )
    before = jnp.cumsum(expert_hits, axis=0) - expert_hits
    slot_rank = jnp.sum(before * expert_hits, axis=1)
    destination = flat_routes * capacity + slot_rank
    table_hits = destination[:, None] == jnp.arange(experts * capacity, dtype=jnp.int32)[None, :]
    return table_hits.astype(jnp.float32).reshape(routes.shape[0], 2, experts * capacity)


def body(
    tokens,
    grad_out,
    expert_ids,
    route_probs,
    gate_up_weight,
    down_weight,
    gate_up_scale_index,
    down_scale_index,
    scale_table,
):
    high = lax.Precision.HIGHEST
    f32 = jnp.float32
    groups = lax.axis_size("expert")
    tok_dev = tokens.shape[0]
    model_width = tokens.shape[1]
    per_device = down_weight.shape[0]
    hidden = down_weight.shape[1]
    experts = per_device * groups
    capacity = 4 * tok_dev // experts
    slots_all = experts * capacity
    slot_hits = slot_tables(expert_ids, experts, capacity)
    either = (slot_hits[:, 0] + slot_hits[:, 1]).astype(jnp.bfloat16)
    row_shape = (groups, per_device, capacity, model_width)
    send_tokens = (
        jnp.einsum("ts,td->sd", either, tokens, preferred_element_type=f32)
        .astype(jnp.bfloat16)
        .reshape(row_shape)
    )
    send_grads = (
        jnp.einsum("ts,td->sd", either, grad_out, preferred_element_type=f32)
        .astype(jnp.bfloat16)
        .reshape(row_shape)
    )
    send_probs = (
        jnp.einsum("tks,tk->s", slot_hits, route_probs.astype(f32), precision=high)
        .astype(jnp.bfloat16)
        .reshape(row_shape[:3])
    )
    recv_tokens, recv_grads, recv_probs = (
        lax.all_to_all(send_tokens, "expert", split_axis=0, concat_axis=0, tiled=True),
        lax.all_to_all(send_grads, "expert", split_axis=0, concat_axis=0, tiled=True),
        lax.all_to_all(send_probs, "expert", split_axis=0, concat_axis=0, tiled=True),
    )
    level_rows = jnp.repeat(lookup(gate_up_scale_index, scale_table), QBLOCK, axis=0)
    full_scale = jnp.repeat(level_rows, hidden, axis=2)
    down_scale = jnp.repeat(lookup(down_scale_index, scale_table), QBLOCK, axis=1)
    down_eff = (down_weight.astype(f32) * down_scale[:, :, None]).astype(jnp.bfloat16)
    gathered = lax.all_gather(gate_up_weight, "dp", axis=0, tiled=True)
    gate_up_eff = (gathered.astype(f32) * full_scale).astype(jnp.bfloat16)
    projected = jnp.einsum("sjcd,djf->sjcf", recv_tokens, gate_up_eff, preferred_element_type=f32)
    gate_part = projected[..., :hidden]
    up_part = projected[..., hidden:]
    sigmoid_gate = jax.nn.sigmoid(gate_part)
    activated = gate_part * sigmoid_gate
    hidden_rows = (activated * up_part).astype(jnp.bfloat16)
    hidden_grad = jnp.einsum("sjcd,jfd->sjcf", recv_grads, down_eff, preferred_element_type=f32)
    probs_wide = recv_probs.astype(f32)[..., None]
    scaled_grad = probs_wide * hidden_grad
    gate_grad = scaled_grad * up_part * sigmoid_gate * (1.0 + gate_part * (1.0 - sigmoid_gate))
    up_grad = scaled_grad * activated
    joint_grad = jnp.concatenate([gate_grad, up_grad], axis=-1).astype(jnp.bfloat16)
    row_grads = jnp.einsum(
        "sjcf,djf->sjcd", joint_grad, gate_up_eff, preferred_element_type=f32
    ).astype(jnp.bfloat16)
    back_rows = lax.all_to_all(row_grads, "expert", split_axis=0, concat_axis=0, tiled=True)
    token_grad = jnp.dot(
        either, back_rows.reshape(slots_all, model_width), preferred_element_type=f32
    ).astype(jnp.bfloat16)
    expert_out = jnp.einsum("sjcf,jfd->sjcd", hidden_rows, down_eff, preferred_element_type=f32)
    back_out = lax.all_to_all(
        expert_out.astype(jnp.bfloat16), "expert", split_axis=0, concat_axis=0, tiled=True
    ).astype(expert_out.dtype)
    picked = jnp.einsum(
        "tks,sd->tkd", slot_hits, back_out.reshape(slots_all, model_width), precision=high
    )
    prob_grad = jnp.sum(picked * grad_out.astype(f32)[:, None, :], axis=-1)
    weighted = (probs_wide * hidden_rows.astype(f32)).astype(jnp.bfloat16)
    partial_sum = jnp.einsum("sjcd,sjcf->djf", recv_tokens, joint_grad, preferred_element_type=f32)
    gate_up_grad = lax.psum_scatter(
        (partial_sum * full_scale).astype(jnp.bfloat16), "dp", scatter_dimension=0, tiled=True
    )
    down_part = (
        jnp.einsum("sjcf,sjcd->jfd", weighted, recv_grads, preferred_element_type=f32)
        * down_scale[:, :, None]
    )
    down_grad = lax.psum(down_part.astype(jnp.bfloat16), "dp")
    return (token_grad, prob_grad, gate_up_grad, down_grad)


def solution(mesh):
    in_specs = (
        P(("dp", "expert"), None),
        P(("dp", "expert"), None),
        P(("dp", "expert"), None),
        P(("dp", "expert"), None),
        P("dp", "expert", None),
        P("expert", None, None),
        P(None, "expert", None),
        P("expert", None),
        P(),
    )
    out_specs = (
        P(("dp", "expert"), None),
        P(("dp", "expert"), None),
        P("dp", "expert", None),
        P("expert", None, None),
    )
    return jax.shard_map(body, mesh=mesh, in_specs=in_specs, out_specs=out_specs, check_vma=False)
```

profile of v0, /device:TPU:2, one launch (start us, length us, event | category | flops | bytes accessed | tf_op | source)
XLA Modules:
  0.0 354.2 jit_solution(2820792020950934844)
XLA Ops:
  12.5 9.4 %all-to-all-start = ((bf16[32,1,16]{2,1,0:T(2,128)(2,1)}), bf16[32,1,16]{2,1,0:T(2,128)(2,1)S(1)}, u32[]{:S(2)}, u32[]{:S(2)}) async-start(bf16[32,1,16]{2,1,0:T(2,128)(2,1)} %reshape.263), calls=%async_computation | async-start | bytes 32768 | tf_op jit(solution)/shard_map/all_to_all | solution.py:70
  22.1 1.4 convolution_convert_fusion.1
  23.5 4.5 %all-to-all-done = bf16[32,1,16]{2,1,0:T(2,128)(2,1)S(1)} async-done(((bf16[32,1,16]{2,1,0:T(2,128)(2,1)}), bf16[32,1,16]{2,1,0:T(2,128)(2,1)S(1)}, u32[]{:S(2)}, u32[]{:S(2)}) %all-to-all-start) | async-done | bytes 1056 | tf_op jit(solution)/shard_map/all_to_all | solution.py:70
  28.0 5.7 %all-to-all-start.2 = ((bf16[32,1,16,1024]{3,2,1,0:T(8,128)(2,1)}), bf16[32,1,16,1024]{3,2,1,0:T(8,128)(2,1)}, u32[]{:S(2)}, u32[]{:S(2)}) async-start(bf16[32,1,16,1024]{3,2,1,0:T(8,128)(2,1)} %bitcast.20), calls=%async_computation.2 | async-start | bytes 2097152 | tf_op jit(solution)/shard_map/all_to_all | solution.py:68
  34.9 1.4 convolution_convert_fusion.2
  36.4 54.6 %all-gather.2.cloned.1.call-done = bf16[1024,1,1536]{2,0,1:T(8,128)(2,1)} async-done(((bf16[64,1,1536]{2,0,1:T(8,128)(2,1)}), bf16[1024,1,1536]{2,0,1:T(8,128)(2,1)}) %all-gather.2.cloned.1.call-update) | async-done | bytes 3145744 | tf_op jit(solution)/shard_map/all_gather | solution.py:76
  91.0 3.2 copy.84
  94.2 7.4 %all-to-all-start.1 = ((bf16[32,1,16,1024]{3,2,1,0:T(8,128)(2,1)}), bf16[32,1,16,1024]{3,2,1,0:T(8,128)(2,1)}, u32[]{:S(2)}, u32[]{:S(2)}) async-start(bf16[32,1,16,1024]{3,2,1,0:T(8,128)(2,1)} %bitcast.158), calls=%async_computation.1 | async-start | bytes 2097152 | tf_op jit(solution)/shard_map/all_to_all | solution.py:69
  102.7 1.2 fusion.3
  103.9 1.7 copy-done.1
  105.5 1.7 copy-done.2
  107.3 5.1 %convolution_bitcast_fusion = f32[32,1,16,1536]{3,0,2,1:T(8,128)} fusion(bf16[1024,1536,1]{0,1,2:T(8,128)(2,1)S(1)} %fusion.3, bf16[32,1,16,1024]{3,2,1,0:T(8,128)(2,1)} %all-to-all-done.2), kind=kOutput, calls=%fused_computation.4 | convolution fusion | flops 1610612736 | bytes 7340032 | tf_op jit(solution)/shard_map/sjcd,djf->sjcf/dot_general | solution.py:78
  112.3 5.5 %all-to-all-done.1 = bf16[32,1,16,1024]{3,2,1,0:T(8,128)(2,1)} async-done(((bf16[32,1,16,1024]{3,2,1,0:T(8,128)(2,1)}), bf16[32,1,16,1024]{3,2,1,0:T(8,128)(2,1)}, u32[]{:S(2)}, u32[]{:S(2)}) %all-to-all-start.1) | async-done | bytes 1048608 | tf_op jit(solution)/shard_map/all_to_all | solution.py:69
  117.8 5.3 %fusion.29 = (bf16[32,16,768]{2,0,1:T(8,128)(2,1)S(1)}, bf16[32,16,768]{2,0,1:T(8,128)(2,1)S(1)}, bf16[32,1,16,768]{3,0,2,1:T(8,128)(2,1)}) fusion(f32[32,1,16,1536]{3,0,2,1:T(8,128)} %convolution_bitcast_fusion, bf16[32,1,16,1024]{3,2,1,0:T(8,128)(2,1)} %all-to-all-done.1, bf16[1,768,1024]{2,1,0:T(8,128)(2,1)S(1)} %copy-done.11, f32[768]{0:T(1024)S(1)} %copy-done.8, ...), kind=kOutput, calls=%fused_computation.46 | convolution fusion | flops 813957120 | bytes 8131584 | tf_op jit(solution)/shard_map/sjcd,jfd->sjcf/dot_general | solution.py:84
  123.2 3.8 %fusion.15 = f32[1536,1024,1]{1,0,2:T(8,128)S(1)} fusion(bf16[32,16,768]{2,0,1:T(8,128)(2,1)S(1)} %get-tuple-element.25, bf16[32,16,768]{2,0,1:T(8,128)(2,1)S(1)} %get-tuple-element.24, bf16[32,1,16,1024]{3,2,1,0:T(8,128)(2,1)} %all-to-all-done.2), kind=kOutput, calls=%fused_computation.33 | convolution fusion | flops 1613758464 | bytes 8912896 | tf_op jit(solution)/shard_map/sjcd,sjcf->djf/dot_general | solution.py:106
  127.0 1.8 fusion.2
  128.8 3.0 copy.104
  131.8 1.4 copy-done.12
  133.4 1.1 fusion.12
  134.5 1.5 copy.94
  136.0 5.7 %all-to-all-start.4 = ((bf16[32,1,16,1024]{3,2,1,0:T(8,128)(2,1)}), bf16[32,1,16,1024]{3,2,1,0:T(8,128)(2,1)}, u32[]{:S(2)}, u32[]{:S(2)}) async-start(bf16[32,1,16,1024]{3,2,1,0:T(8,128)(2,1)} %copy.94), calls=%async_computation.4 | async-start | bytes 2097152 | tf_op jit(solution)/shard_map/all_to_all | solution.py:98
  142.0 4.1 %fusion.11 = bf16[1,768,1024]{2,1,0:T(8,128)(2,1)} fusion(f32[768]{0:T(1024)S(1)} %copy-done.8, bf16[32,1,16,1024]{3,2,1,0:T(8,128)(2,1)} %all-to-all-done.1, bf16[32,1,16,768]{3,0,2,1:T(8,128)(2,1)} %get-tuple-element.26, f32[32,16]{0,1:T(8,128)S(1)} %copy.86), kind=kOutput, calls=%fused_computation.23 | convolution fusion | flops 808058880 | bytes 3412992 | tf_op jit(solution)/shard_map/sjcf,sjcd->jfd/dot_general | solution.py:111
  146.2 3.2 fusion.13
  149.3 1.6 copy.93
  150.9 7.1 %all-to-all-done.4 = bf16[32,1,16,1024]{3,2,1,0:T(8,128)(2,1)} async-done(((bf16[32,1,16,1024]{3,2,1,0:T(8,128)(2,1)}), bf16[32,1,16,1024]{3,2,1,0:T(8,128)(2,1)}, u32[]{:S(2)}, u32[]{:S(2)}) %all-to-all-start.4) | async-done | bytes 1048608 | tf_op jit(solution)/shard_map/all_to_all | solution.py:98
  158.0 5.0 %all-to-all-start.3 = ((bf16[32,1,16,1024]{3,2,1,0:T(8,128)(2,1)}), bf16[32,1,16,1024]{3,2,1,0:T(8,128)(2,1)S(1)}, u32[]{:S(2)}, u32[]{:S(2)}) async-start(bf16[32,1,16,1024]{3,2,1,0:T(8,128)(2,1)} %copy.93), calls=%async_computation.3 | async-start | bytes 2097152 | tf_op jit(solution)/shard_map/all_to_all | solution.py:93
  163.1 2.4 fusion.14
  165.5 13.8 %all-to-all-done.3 = bf16[32,1,16,1024]{3,2,1,0:T(8,128)(2,1)S(1)} async-done(((bf16[32,1,16,1024]{3,2,1,0:T(8,128)(2,1)}), bf16[32,1,16,1024]{3,2,1,0:T(8,128)(2,1)S(1)}, u32[]{:S(2)}, u32[]{:S(2)}) %all-to-all-start.3) | async-done | bytes 1048608 | tf_op jit(solution)/shard_map/all_to_all | solution.py:93
  180.3 22.1 %reduce-scatter.4.cloned.1.call-done = bf16[64,1536]{1,0:T(8,128)(2,1)} async-done(((bf16[1024,1536]{1,0:T(8,128)(2,1)}), bf16[64,1536]{1,0:T(8,128)(2,1)}) %reduce-scatter.4.cloned.1.call-update) | async-done | bytes 196624
  202.4 1.1 copy.105
  204.4 140.6 %all-reduce.2.cloned.1.call-done = bf16[1,768,1024]{2,1,0:T(8,128)(2,1)} async-done(((bf16[1,768,1024]{2,1,0:T(8,128)(2,1)}), bf16[1,768,1024]{2,1,0:T(8,128)(2,1)}) %all-reduce.2.cloned.1.call-update) | async-done | bytes 1572880 | tf_op jit(solution)/shard_map/psum | solution.py:114
  345.0 2.7 copy.132
  (71 shorter events, 10.0 us)
Async XLA Ops:
  7.2 14.9 %copy-start = (bf16[128,1024]{1,0:T(8,128)(2,1)S(1)}, bf16[128,1024]{1,0:T(8,128)(2,1)}, u32[]{:S(2)}) copy-start(bf16[128,1024]{1,0:T(8,128)(2,1)} %param.9) | copy-start | bytes 786436
  7.2 83.8 %all-gather.2.cloned.1.call-start = ((), (), s32[]{:S(2)}) async-start(), calls=%async_computation.6 | async-start | bytes 3342336 | tf_op jit(solution)/shard_map/all_gather | solution.py:76
  10.8 11.0 %copy-start.6 = (s32[128,2]{0,1:T(2,128)}, s32[128,2]{0,1:T(2,128)S(1)}, u32[]{:S(2)}) copy-start(s32[128,2]{0,1:T(2,128)S(1)} %multiply_add_fusion) | copy-start | bytes 3076
  12.5 15.6 %all-to-all-start = ((bf16[32,1,16]{2,1,0:T(2,128)(2,1)}), bf16[32,1,16]{2,1,0:T(2,128)(2,1)S(1)}, u32[]{:S(2)}, u32[]{:S(2)}) async-start(bf16[32,1,16]{2,1,0:T(2,128)(2,1)} %reshape.263), calls=%async_computation | async-start | bytes 32768 | tf_op jit(solution)/shard_map/all_to_all | solution.py:70
  22.0 11.8 %copy-start.9 = (s32[8,1,2]{0,2,1:T(2,128)S(1)}, s32[8,1,2]{0,2,1:T(2,128)}, u32[]{:S(2)}) copy-start(s32[8,1,2]{0,2,1:T(2,128)} %param.15) | copy-start | bytes 196
  22.0 11.8 %copy-start.10 = (f32[16]{0:T(128)S(1)}, f32[16]{0:T(128)}, u32[]{:S(2)}) copy-start(f32[16]{0:T(128)} %param.17) | copy-start | bytes 196
  22.0 12.0 %copy-start.13 = (s32[1,6]{1,0:T(1,128)S(1)}, s32[1,6]{1,0:T(1,128)}, u32[]{:S(2)}) copy-start(s32[1,6]{1,0:T(1,128)} %param.16) | copy-start | bytes 76
  22.0 12.9 %copy-start.4 = (bf16[128,1024]{1,0:T(8,128)(2,1)S(1)}, bf16[128,1024]{1,0:T(8,128)(2,1)}, u32[]{:S(2)}) copy-start(bf16[128,1024]{1,0:T(8,128)(2,1)} %param.10) | copy-start | bytes 786436
  28.0 66.2 %all-to-all-start.2 = ((bf16[32,1,16,1024]{3,2,1,0:T(8,128)(2,1)}), bf16[32,1,16,1024]{3,2,1,0:T(8,128)(2,1)}, u32[]{:S(2)}, u32[]{:S(2)}) async-start(bf16[32,1,16,1024]{3,2,1,0:T(8,128)(2,1)} %bitcast.20), calls=%async_computation.2 | async-start | bytes 2097152 | tf_op jit(solution)/shard_map/all_to_all | solution.py:68
  94.2 23.6 %all-to-all-start.1 = ((bf16[32,1,16,1024]{3,2,1,0:T(8,128)(2,1)}), bf16[32,1,16,1024]{3,2,1,0:T(8,128)(2,1)}, u32[]{:S(2)}, u32[]{:S(2)}) async-start(bf16[32,1,16,1024]{3,2,1,0:T(8,128)(2,1)} %bitcast.158), calls=%async_computation.1 | async-start | bytes 2097152 | tf_op jit(solution)/shard_map/all_to_all | solution.py:69
  101.7 100.8 %reduce-scatter.4.cloned.1.call-start = ((), (), s32[]{:S(2)}) async-start(), calls=%async_computation.8 | async-start | bytes 3342336
  102.7 2.9 copy-start.1
  105.5 1.7 copy-start.2
  107.3 10.6 %copy-start.8 = (f32[768]{0:T(1024)S(1)}, f32[768]{0:T(1024)}, u32[]{:S(2)}) copy-start(f32[768]{0:T(1024)} %broadcast_bitcast_fusion.1) | copy-start | bytes 9220
  107.3 10.6 %copy-start.11 = (bf16[1,768,1024]{2,1,0:T(8,128)(2,1)S(1)}, bf16[1,768,1024]{2,1,0:T(8,128)(2,1)}, u32[]{:S(2)}) copy-start(bf16[1,768,1024]{2,1,0:T(8,128)(2,1)} %param.14) | copy-start | bytes 4718596
  117.8 9.2 %slice-start = ((s8[6291456]{0:T(1024)(128)(4,1)}), s8[4194304]{0:T(1024)(128)(4,1)S(1)}, s32[]{:S(2)}) async-start(s8[6291456]{0:T(1024)(128)(4,1)} %bitcast.155), calls=%async_computation.9 | async-start | bytes 8388608
  123.1 3.8 %copy-start.15 = (bf16[32,16,768]{2,0,1:T(8,128)(2,1)}, bf16[32,16,768]{2,0,1:T(8,128)(2,1)S(1)}, u32[]{:S(2)}) copy-start(bf16[32,16,768]{2,0,1:T(8,128)(2,1)S(1)} %get-tuple-element.24) | copy-start | bytes 2359300
  123.1 3.8 %copy-start.16 = (bf16[32,16,768]{2,0,1:T(8,128)(2,1)}, bf16[32,16,768]{2,0,1:T(8,128)(2,1)S(1)}, u32[]{:S(2)}) copy-start(bf16[32,16,768]{2,0,1:T(8,128)(2,1)S(1)} %get-tuple-element.25) | copy-start | bytes 2359300
  123.1 3.9 %slice-start.1 = ((s8[6291456]{0:T(1024)(128)(4,1)}), s8[2097152]{0:T(1024)(128)(4,1)S(1)}, s32[]{:S(2)}) async-start(s8[6291456]{0:T(1024)(128)(4,1)} %bitcast.155), calls=%async_computation.10 | async-start | bytes 4194304
  131.8 1.4 copy-start.12
  131.8 1.6 copy-start.14
  136.0 22.0 %all-to-all-start.4 = ((bf16[32,1,16,1024]{3,2,1,0:T(8,128)(2,1)}), bf16[32,1,16,1024]{3,2,1,0:T(8,128)(2,1)}, u32[]{:S(2)}, u32[]{:S(2)}) async-start(bf16[32,1,16,1024]{3,2,1,0:T(8,128)(2,1)} %copy.94), calls=%async_computation.4 | async-start | bytes 2097152 | tf_op jit(solution)/shard_map/all_to_all | solution.py:98
  141.8 4.4 %copy-start.3 = (bf16[1024,1536,1]{0,1,2:T(8,128)(2,1)S(1)}, bf16[1024,1536,1]{0,1,2:T(8,128)(2,1)}, u32[]{:S(2)}) copy-start(bf16[1024,1536,1]{0,1,2:T(8,128)(2,1)} %copy-done.2) | copy-start | bytes 9437188
  141.8 203.2 %all-reduce.2.cloned.1.call-start = ((), (), s32[]{:S(2)}) async-start(), calls=%async_computation.7 | async-start | bytes 3145728 | tf_op jit(solution)/shard_map/psum | solution.py:114
  149.3 13.7 %copy-start.5 = (bf16[128,1024]{1,0:T(8,128)(2,1)S(1)}, bf16[128,1024]{1,0:T(8,128)(2,1)}, u32[]{:S(2)}) copy-start(bf16[128,1024]{1,0:T(8,128)(2,1)} %param.10) | copy-start | bytes 786436
  149.3 13.8 %copy-start.7 = (s32[128,2]{0,1:T(2,128)S(1)}, s32[128,2]{0,1:T(2,128)}, u32[]{:S(2)}) copy-start(s32[128,2]{0,1:T(2,128)} %copy-done.6) | copy-start | bytes 3076
  158.0 21.3 %all-to-all-start.3 = ((bf16[32,1,16,1024]{3,2,1,0:T(8,128)(2,1)}), bf16[32,1,16,1024]{3,2,1,0:T(8,128)(2,1)S(1)}, u32[]{:S(2)}, u32[]{:S(2)}) async-start(bf16[32,1,16,1024]{3,2,1,0:T(8,128)(2,1)} %copy.93), calls=%async_computation.3 | async-start | bytes 2097152 | tf_op jit(solution)/shard_map/all_to_all | solution.py:93
Sparse Core Ops, SparseCore 0:
  10.1 80.8 all-gather.1
  131.9 70.4 reduce-scatter.3
  205.3 139.6 all-reduce.1
where the time goes:
time: 355 us; the launch traced here: 354 us
  waiting for transfers between devices  249 us (70%)
  starting transfers between devices  33.8 us (10%)
  matrix products  29.7 us (8%)
  local copies, waits for them, and re-layouts  22.7 us (6%)
  between operations  14.1 us (4%)
  other arithmetic  4.95 us (1%)
    psum x1, waiting for transfers between devices, body(): down_grad = lax.psum(down_part.astype(jnp.bfloat16), 'dp')  141 us
    all_gather x1, waiting for transfers between devices, body(): gathered = lax.all_gather(gate_up_weight, 'dp', axis=0, tiled=True)  54.6 us
    unnamed x4, waiting for transfers between devices  22.8 us
    all_to_all x1, waiting for transfers between devices, body(): lax.all_to_all(row_grads, 'expert', split_axis=0, concat_axis=0, tiled=True)  13.8 us
    unnamed x45, local copies, waits for them, and re-layouts  13.5 us
    all_to_all x1, starting transfers between devices, body(): lax.all_to_all(send_probs, 'expert', split_axis=0, concat_axis=0, tiled=T...  9.4 us
    all_to_all x1, starting transfers between devices, body(): lax.all_to_all(send_grads, 'expert', split_axis=0, concat_axis=0, tiled=T...  7.43 us
  transfers between devices with their start and end apart: 8, of which 7 were waited for; matrix products, arithmetic and copies ran while one was open for 10% of the time, Pallas kernels for 0%

commit v1 on v0

--- a/solution.py
+++ b/solution.py
@@ -4,6 +4,11 @@
 from jax.sharding import PartitionSpec as P
 
 QBLOCK = 128
+
+
+def add_all(x, mesh_axis):
+    parts = lax.all_gather(x, mesh_axis)
+    return jnp.sum(parts, axis=0)
 
 
 def lookup(level_index, level_table):
@@ -111,7 +116,7 @@
         jnp.einsum("sjcf,sjcd->jfd", weighted, recv_grads, preferred_element_type=f32)
         * down_scale[:, :, None]
     )
-    down_grad = lax.psum(down_part.astype(jnp.bfloat16), "dp")
+    down_grad = add_all(down_part.astype(jnp.bfloat16), "dp")
     return (token_grad, prob_grad, gate_up_grad, down_grad)
 
 

time: 355 us -> 500 us (1.41)
  the two profiles are of different devices: /device:TPU:2 before, /device:TPU:1 now
where the time goes in v1:
time: 500 us; the launch traced here: 499 us
  waiting for transfers between devices  376 us (75%)
  starting transfers between devices  40.7 us (8%)
  matrix products  29.3 us (6%)
  other arithmetic  19.9 us (4%)
  local copies, waits for them, and re-layouts  19 us (4%)
  between operations  14.1 us (3%)
    all_gather x1, waiting for transfers between devices, add_all(): parts = lax.all_gather(x, mesh_axis)  282 us
    all_gather x1, waiting for transfers between devices, body(): gathered = lax.all_gather(gate_up_weight, 'dp', axis=0, tiled=True)  46.3 us
    all_to_all x1, starting transfers between devices, body(): lax.all_to_all(send_grads, 'expert', split_axis=0, concat_axis=0, tiled=T...  16.3 us
    reduce_sum x1, other arithmetic, add_all(): return jnp.sum(parts, axis=0)  14.9 us
    all_to_all x1, waiting for transfers between devices, body(): lax.all_to_all(row_grads, 'expert', split_axis=0, concat_axis=0, tiled=True)  14.9 us
    all_to_all x1, waiting for transfers between devices, body(): lax.all_to_all(expert_out.astype(jnp.bfloat16), 'expert', split_axis=0, c...  12.5 us
    all_to_all x1, starting transfers between devices, body(): lax.all_to_all(send_probs, 'expert', split_axis=0, concat_axis=0, tiled=T...  10.4 us
    unnamed x40, local copies, waits for them, and re-layouts  10.3 us
  transfers between devices with their start and end apart: 8, of which 7 were waited for; matrix products, arithmetic and copies ran while one was open for 7% of the time, Pallas kernels for 0%

profile of v1, /device:TPU:1, one launch (start us, length us, event | category | flops | bytes accessed | tf_op | source)
XLA Modules:
  0.0 499.3 jit_solution(16903885732738212160)
XLA Ops:
  12.5 10.4 %all-to-all-start = ((bf16[32,1,16]{2,1,0:T(2,128)(2,1)}), bf16[32,1,16]{2,1,0:T(2,128)(2,1)S(1)}, u32[]{:S(2)}, u32[]{:S(2)}) async-start(bf16[32,1,16]{2,1,0:T(2,128)(2,1)} %reshape.267), calls=%async_computation | async-start | bytes 32768 | tf_op jit(solution)/shard_map/all_to_all | solution.py:75
  23.0 1.4 convolution_convert_fusion.1
  24.5 5.3 %all-to-all-done = bf16[32,1,16]{2,1,0:T(2,128)(2,1)S(1)} async-done(((bf16[32,1,16]{2,1,0:T(2,128)(2,1)}), bf16[32,1,16]{2,1,0:T(2,128)(2,1)S(1)}, u32[]{:S(2)}, u32[]{:S(2)}) %all-to-all-start) | async-done | bytes 1056 | tf_op jit(solution)/shard_map/all_to_all | solution.py:75
  29.8 4.9 all-to-all-start.2
  35.2 1.5 convolution_convert_fusion.2
  36.8 46.3 %all-gather.4.cloned.1.call-done = bf16[1024,1,1536]{2,0,1:T(8,128)(2,1)} async-done(((bf16[64,1,1536]{2,0,1:T(8,128)(2,1)}), bf16[1024,1,1536]{2,0,1:T(8,128)(2,1)}) %all-gather.4.cloned.1.call-update) | async-done | bytes 3145744 | tf_op jit(solution)/shard_map/all_gather | solution.py:81
  83.0 3.2 copy.84
  86.2 16.3 %all-to-all-start.1 = ((bf16[32,1,16,1024]{3,2,1,0:T(8,128)(2,1)}), bf16[32,1,16,1024]{3,2,1,0:T(8,128)(2,1)}, u32[]{:S(2)}, u32[]{:S(2)}) async-start(bf16[32,1,16,1024]{3,2,1,0:T(8,128)(2,1)} %bitcast.157), calls=%async_computation.1 | async-start | bytes 2097152 | tf_op jit(solution)/shard_map/all_to_all | solution.py:74
  103.6 1.2 fusion.3
  104.8 1.7 copy-done.2
  106.5 1.7 copy-done.3
  108.2 5.1 %convolution_bitcast_fusion = f32[32,1,16,1536]{3,0,2,1:T(8,128)} fusion(bf16[1024,1536,1]{0,1,2:T(8,128)(2,1)S(1)} %fusion.3, bf16[32,1,16,1024]{3,2,1,0:T(8,128)(2,1)} %all-to-all-done.2), kind=kOutput, calls=%fused_computation.4 | convolution fusion | flops 1610612736 | bytes 7340032 | tf_op jit(solution)/shard_map/sjcd,djf->sjcf/dot_general | solution.py:83
  113.3 6.5 %all-to-all-done.1 = bf16[32,1,16,1024]{3,2,1,0:T(8,128)(2,1)} async-done(((bf16[32,1,16,1024]{3,2,1,0:T(8,128)(2,1)}), bf16[32,1,16,1024]{3,2,1,0:T(8,128)(2,1)}, u32[]{:S(2)}, u32[]{:S(2)}) %all-to-all-start.1) | async-done | bytes 1048608 | tf_op jit(solution)/shard_map/all_to_all | solution.py:74
  119.8 5.3 %fusion.28 = (bf16[32,16,768]{2,0,1:T(8,128)(2,1)S(1)}, bf16[32,16,768]{2,0,1:T(8,128)(2,1)S(1)}, bf16[32,1,16,768]{3,0,2,1:T(8,128)(2,1)}) fusion(f32[32,1,16,1536]{3,0,2,1:T(8,128)} %convolution_bitcast_fusion, bf16[32,1,16,1024]{3,2,1,0:T(8,128)(2,1)} %all-to-all-done.1, bf16[1,768,1024]{2,1,0:T(8,128)(2,1)S(1)} %copy-done.9, ...), kind=kOutput, calls=%fused_computation.45 | convolution fusion | flops 813957120 | bytes 8131584 | tf_op jit(solution)/shard_map/sjcd,jfd->sjcf/dot_general | solution.py:89
  125.1 3.8 fusion.14
  129.0 1.8 fusion.2
  130.8 2.9 copy.104
  133.8 1.1 copy-done.12
  134.9 3.7 fusion.4
  138.6 1.1 fusion.11
  139.7 1.6 copy.94
  141.2 4.9 all-to-all-start.4
  146.1 3.2 fusion.12
  149.3 1.6 copy.93
  150.9 12.5 %all-to-all-done.4 = bf16[32,1,16,1024]{3,2,1,0:T(8,128)(2,1)} async-done(((bf16[32,1,16,1024]{3,2,1,0:T(8,128)(2,1)}), bf16[32,1,16,1024]{3,2,1,0:T(8,128)(2,1)}, u32[]{:S(2)}, u32[]{:S(2)}) %all-to-all-start.4) | async-done | bytes 1048608 | tf_op jit(solution)/shard_map/all_to_all | solution.py:103
  163.4 4.0 all-to-all-start.3
  167.5 2.4 fusion.13
  169.8 14.9 %all-to-all-done.3 = bf16[32,1,16,1024]{3,2,1,0:T(8,128)(2,1)S(1)} async-done(((bf16[32,1,16,1024]{3,2,1,0:T(8,128)(2,1)}), bf16[32,1,16,1024]{3,2,1,0:T(8,128)(2,1)S(1)}, u32[]{:S(2)}, u32[]{:S(2)}) %all-to-all-start.3) | async-done | bytes 1048608 | tf_op jit(solution)/shard_map/all_to_all | solution.py:98
  185.7 8.4 %reduce-scatter.4.cloned.1.call-done = bf16[64,1536]{1,0:T(8,128)(2,1)} async-done(((bf16[1024,1536]{1,0:T(8,128)(2,1)}), bf16[64,1536]{1,0:T(8,128)(2,1)}) %reduce-scatter.4.cloned.1.call-update) | async-done | bytes 196624
  194.2 1.1 copy.105
  196.2 281.7 %all-gather.6.cloned.1.call-done = bf16[12288,1024]{1,0:T(8,128)(2,1)} async-done(((bf16[768,1024]{1,0:T(8,128)(2,1)}), bf16[12288,1024]{1,0:T(8,128)(2,1)}) %all-gather.6.cloned.1.call-update) | async-done | bytes 25165840 | tf_op jit(solution)/shard_map/all_gather | solution.py:10
  477.9 14.9 %reduce.4 = bf16[768,1024]{1,0:T(8,128)(2,1)} reduce(bf16[16,768,1024]{2,1,0:T(8,128)(2,1)} %bitcast.156, bf16[]{:T(256)} %constant.15.clone.1), dimensions={0}, to_apply=%region_7.8 | reduce | flops 11796480 | bytes 26738690 | tf_op jit(solution)/shard_map/reduce_sum | solution.py:11
  (67 shorter events, 9.0 us)
Async XLA Ops:
  7.2 15.9 %copy-start = (bf16[128,1024]{1,0:T(8,128)(2,1)S(1)}, bf16[128,1024]{1,0:T(8,128)(2,1)}, u32[]{:S(2)}) copy-start(bf16[128,1024]{1,0:T(8,128)(2,1)} %param.9) | copy-start | bytes 786436
  7.2 75.9 %all-gather.4.cloned.1.call-start = ((), (), s32[]{:S(2)}) async-start(), calls=%async_computation.6 | async-start | bytes 3342336 | tf_op jit(solution)/shard_map/all_gather | solution.py:81
  12.5 17.3 %all-to-all-start = ((bf16[32,1,16]{2,1,0:T(2,128)(2,1)}), bf16[32,1,16]{2,1,0:T(2,128)(2,1)S(1)}, u32[]{:S(2)}, u32[]{:S(2)}) async-start(bf16[32,1,16]{2,1,0:T(2,128)(2,1)} %reshape.267), calls=%async_computation | async-start | bytes 32768 | tf_op jit(solution)/shard_map/all_to_all | solution.py:75
  22.9 11.8 %copy-start.7 = (s32[8,1,2]{0,2,1:T(2,128)S(1)}, s32[8,1,2]{0,2,1:T(2,128)}, u32[]{:S(2)}) copy-start(s32[8,1,2]{0,2,1:T(2,128)} %param.15) | copy-start | bytes 196
  23.0 11.8 %copy-start.8 = (f32[16]{0:T(128)S(1)}, f32[16]{0:T(128)}, u32[]{:S(2)}) copy-start(f32[16]{0:T(128)} %param.17) | copy-start | bytes 196
  23.0 12.0 %copy-start.11 = (s32[1,6]{1,0:T(1,128)S(1)}, s32[1,6]{1,0:T(1,128)}, u32[]{:S(2)}) copy-start(s32[1,6]{1,0:T(1,128)} %param.16) | copy-start | bytes 76
  23.0 12.3 %copy-start.5 = (bf16[128,1024]{1,0:T(8,128)(2,1)S(1)}, bf16[128,1024]{1,0:T(8,128)(2,1)}, u32[]{:S(2)}) copy-start(bf16[128,1024]{1,0:T(8,128)(2,1)} %param.10) | copy-start | bytes 786436
  29.8 56.4 %all-to-all-start.2 = ((bf16[32,1,16,1024]{3,2,1,0:T(8,128)(2,1)}), bf16[32,1,16,1024]{3,2,1,0:T(8,128)(2,1)}, u32[]{:S(2)}, u32[]{:S(2)}) async-start(bf16[32,1,16,1024]{3,2,1,0:T(8,128)(2,1)} %bitcast.20), calls=%async_computation.2 | async-start | bytes 2097152 | tf_op jit(solution)/shard_map/all_to_all | solution.py:73
  86.2 33.6 %all-to-all-start.1 = ((bf16[32,1,16,1024]{3,2,1,0:T(8,128)(2,1)}), bf16[32,1,16,1024]{3,2,1,0:T(8,128)(2,1)}, u32[]{:S(2)}, u32[]{:S(2)}) async-start(bf16[32,1,16,1024]{3,2,1,0:T(8,128)(2,1)} %bitcast.157), calls=%async_computation.1 | async-start | bytes 2097152 | tf_op jit(solution)/shard_map/all_to_all | solution.py:74
  102.6 91.6 %reduce-scatter.4.cloned.1.call-start = ((), (), s32[]{:S(2)}) async-start(), calls=%async_computation.8 | async-start | bytes 3342336
  103.6 2.9 copy-start.2
  106.5 1.7 copy-start.3
  108.2 11.6 %copy-start.9 = (bf16[1,768,1024]{2,1,0:T(8,128)(2,1)S(1)}, bf16[1,768,1024]{2,1,0:T(8,128)(2,1)}, u32[]{:S(2)}) copy-start(bf16[1,768,1024]{2,1,0:T(8,128)(2,1)} %param.14) | copy-start | bytes 4718596
  119.8 9.2 %slice-start = ((s8[6291456]{0:T(1024)(128)(4,1)}), s8[4194304]{0:T(1024)(128)(4,1)S(1)}, s32[]{:S(2)}) async-start(s8[6291456]{0:T(1024)(128)(4,1)} %bitcast.153), calls=%async_computation.9 | async-start | bytes 8388608
  125.1 3.8 copy-start.13
  125.1 3.8 copy-start.14
  125.1 3.9 slice-start.1
  133.7 1.1 copy-start.12
  133.7 344.1 %all-gather.6.cloned.1.call-start = ((), (), s32[]{:S(2)}) async-start(), calls=%async_computation.7 | async-start | bytes 26738688 | tf_op jit(solution)/shard_map/all_gather | solution.py:10
  134.8 3.7 copy-start.10
  139.7 6.4 %copy-start.4 = (bf16[1024,1536,1]{0,1,2:T(8,128)(2,1)S(1)}, bf16[1024,1536,1]{0,1,2:T(8,128)(2,1)}, u32[]{:S(2)}) copy-start(bf16[1024,1536,1]{0,1,2:T(8,128)(2,1)} %copy-done.3) | copy-start | bytes 9437188
  141.2 22.2 %all-to-all-start.4 = ((bf16[32,1,16,1024]{3,2,1,0:T(8,128)(2,1)}), bf16[32,1,16,1024]{3,2,1,0:T(8,128)(2,1)}, u32[]{:S(2)}, u32[]{:S(2)}) async-start(bf16[32,1,16,1024]{3,2,1,0:T(8,128)(2,1)} %copy.94), calls=%async_computation.4 | async-start | bytes 2097152 | tf_op jit(solution)/shard_map/all_to_all | solution.py:103
  149.3 18.1 %copy-start.6 = (bf16[128,1024]{1,0:T(8,128)(2,1)S(1)}, bf16[128,1024]{1,0:T(8,128)(2,1)}, u32[]{:S(2)}) copy-start(bf16[128,1024]{1,0:T(8,128)(2,1)} %param.10) | copy-start | bytes 786436
  163.4 21.3 %all-to-all-start.3 = ((bf16[32,1,16,1024]{3,2,1,0:T(8,128)(2,1)}), bf16[32,1,16,1024]{3,2,1,0:T(8,128)(2,1)S(1)}, u32[]{:S(2)}, u32[]{:S(2)}) async-start(bf16[32,1,16,1024]{3,2,1,0:T(8,128)(2,1)} %copy.93), calls=%async_computation.3 | async-start | bytes 2097152 | tf_op jit(solution)/shard_map/all_to_all | solution.py:98
  477.9 14.9 %copy-start.1 = (bf16[128,1024]{1,0:T(8,128)(2,1)S(1)}, bf16[128,1024]{1,0:T(8,128)(2,1)}, u32[]{:S(2)}) copy-start(bf16[128,1024]{1,0:T(8,128)(2,1)} %param.9) | copy-start | bytes 786436
Sparse Core Ops, SparseCore 0:
  10.1 72.9 all-gather.3
  133.9 60.2 reduce-scatter.3
  196.8 281.0 all-gather.5
